TPU v7x, 32 devices: a whole 2x2x4 slice. The times are simulated.
32 devices in a mesh: snap: 4 (over y, x), sp: 8 (over z, core).
Axes of the slice: x: 2, y: 2, z: 4, core: 2. Of those that a mesh axis runs over, the one named last changes fastest.
Arguments:
- fields: bfloat16 [16, 16, 180, 768], P('snap', 'sp'), may hold values from -6 to 6
- cotangent: bfloat16 [16, 16, 180, 768], P('snap', 'sp'), may hold values from -6 to 6
- valid_mask: int32 [16, 16, 180], P('snap', 'sp'), may hold values from 0 to 1, as said below
- kept_modes: int32 [16, 8], P(None, 'sp'), may hold values 0 or 1
- mlp_master: float32 [2, 768, 3072], P(None, 'sp'), may hold values from -0.21875 to 0.21875
- mlp_first: float32 [2, 768, 3072], P(None, 'sp'), may hold values from -384 to 384
- mlp_second: float32 [2, 768, 3072], P(None, 'sp'), may hold values from 2304 to 18432
- filter_master: float32 [4, 768, 96], P(None, 'sp'), may hold values from -1.25 to 1.25
- filter_first: float32 [4, 768, 96], P(None, 'sp'), may hold values from -448 to 448
- filter_second: float32 [4, 768, 96], P(None, 'sp'), may hold values from 2048 to 16384
- small_master: float32 [13, 768], P(None, 'sp'), may hold values from -1.2 to 1.8, as said below
- small_first: float32 [13, 768], P(None, 'sp'), may hold values from -896 to 896
- small_second: float32 [13, 768], P(None, 'sp'), may hold values from 4608 to 92160
- run_stats: float32 [2, 20], replicated, may hold values from -6 to 6
Outputs:
- block_out: bfloat16 [16, 16, 180, 768], P('snap', 'sp')
- input_grad: float32 [16, 16, 180, 768], P('snap', 'sp')
- mlp_new: float32 [2, 768, 3072], P(None, 'sp')
- mlp_first_new: float32 [2, 768, 3072], P(None, 'sp')
- mlp_second_new: float32 [2, 768, 3072], P(None, 'sp')
- mlp_copy: bfloat16 [2, 768, 3072], P(None, 'sp')
- filter_new: float32 [4, 768, 96], P(None, 'sp')
- filter_first_new: float32 [4, 768, 96], P(None, 'sp')
- filter_second_new: float32 [4, 768, 96], P(None, 'sp')
- filter_copy: bfloat16 [4, 768, 96], P(None, 'sp')
- small_new: float32 [13, 768], P(None, 'sp')
- small_first_new: float32 [13, 768], P(None, 'sp')
- small_second_new: float32 [13, 768], P(None, 'sp')
- small_copy: bfloat16 [13, 768], P(None, 'sp')
- stats_new: float32 [2, 20], replicated
Inputs may be any that keep to these rules, and one draw needn't show every extreme that they name: `valid_mask`: the first longitude of every row is valid. `small_master`: gains (rows 0 and 2) lie about 1, the other rows about 0.
All inputs are finite; a program needn't handle non-finite values. No bound on the sum of `kept_modes` on one device may be relied on, other than what follows from the above.
Results may differ from a plain program's by a relative error of at most 0.025.
The roundings to bfloat16 on the way count: a program that leaves them out, or rounds other values in their place, can miss the bound.
Values may be sent and summed in bfloat16 or wider, within the bound.
A program may use at most 192 MiB of HBM per device.

v0:
```python
import functools
import math

import jax
import jax.numpy as jnp
import ml_dtypes
import numpy as np
from jax import lax
from jax.experimental import pallas as pl
from jax.experimental.pallas import tpu as pltpu
from jax.sharding import PartitionSpec as P

BLOCKS = 8
NVAR = 20
STEP = 10
VMEM_LIMIT = 63 * 1024 * 1024


eps_norm = 1e-06
shrink_level = 0.01
beta_one = 0.5
beta_two = 0.5
adam_eps = 1e-08
decay_rate = 0.01
rate_mlp = 0.03
rate_filter = 0.1
rate_small = 0.2
stat_decay = 0.5


def layer_norm(values, gain_vec, shift_vec):
    centred = values - jnp.mean(values, axis=-1, keepdims=True)
    spread = jnp.mean(centred * centred, axis=-1, keepdims=True)
    return centred * lax.rsqrt(spread + eps_norm) * gain_vec + shift_vec


def shrink(values):
    return values - shrink_level * jnp.tanh(values / shrink_level)


def lon_tables(lon_total, mode_total):
    places = jnp.arange(lon_total, dtype=jnp.int32)
    orders = jnp.arange(mode_total, dtype=jnp.int32)
    angles = (places[:, None] * orders[None, :] % lon_total).astype(jnp.float32) * (
        2.0 * math.pi / lon_total
    )
    scaling = 1.0 / math.sqrt(lon_total)
    forward_tab = jnp.stack([jnp.cos(angles), -jnp.sin(angles)], axis=1) * scaling
    doubling = jnp.where(orders == 0, 1.0, 2.0).astype(jnp.float32)[:, None]
    inverse_tab = (
        jnp.stack([jnp.cos(angles).T * doubling, -jnp.sin(angles).T * doubling], axis=0) * scaling
    )
    return (forward_tab.astype(jnp.bfloat16), inverse_tab.astype(jnp.bfloat16))


def lat_table(lat_total):
    places = jnp.arange(lat_total, dtype=jnp.int32)
    angles = (places[:, None] * places[None, :] % lat_total).astype(jnp.float32) * (
        2.0 * math.pi / lat_total
    )
    cosine = jnp.cos(angles)
    sine_part = jnp.sin(angles)
    upper_rows = jnp.stack([cosine, sine_part], axis=1)
    bottom = jnp.stack([-sine_part, cosine], axis=1)
    return (jnp.stack([upper_rows, bottom], axis=0) / math.sqrt(lat_total)).astype(jnp.bfloat16)


def complex_pair(real_part, imag_part):
    return jnp.stack([jnp.stack([real_part, -imag_part]), jnp.stack([imag_part, real_part])])


gelu_scale = math.sqrt(2.0 / math.pi)
gelu_cubic = 0.044715


def gelu_both(value):
    bend = (gelu_scale * gelu_cubic) * (value * value)
    turn = jnp.tanh(value * (gelu_scale + bend))
    half = 0.5 + 0.5 * turn
    slope = half * (1.0 + (value * (1.0 - turn)) * (gelu_scale + 3.0 * bend))
    return value * half, slope


def dot_nt(left, right):
    return lax.dot_general(
        left, right, (((1,), (1,)), ((), ())), preferred_element_type=jnp.float32
    )


def dot_nn(left, right):
    return jnp.dot(left, right, preferred_element_type=jnp.float32)


def divisor(total, unit, most):
    return max(size for size in range(unit, most + 1, unit) if total % size == 0)


def mlp_body(
    tile,
    normed_ref,
    cot_ref,
    up_ref,
    down_ref,
    bias_ref,
    out_ref,
    back_ref,
    grad_up_ref,
    grad_down_ref,
    grad_bias_ref,
    normed_turned,
    cot_turned,
    act_ref,
    slope_ref,
):
    tokens = normed_ref.shape[0]

    @pl.when(pl.program_id(0) == 0)
    def _():
        normed_turned[...] = normed_ref[...].T
        cot_turned[...] = cot_ref[...].T
        out_ref[...] = jnp.zeros_like(out_ref)
        back_ref[...] = jnp.zeros_like(back_ref)

    grad_bias_ref[...] = jnp.zeros_like(grad_bias_ref)

    @pl.loop(0, tokens // tile)
    def _(step):
        rows = pl.ds(pl.multiple_of(step * tile, tile), tile)
        act, slope = gelu_both(dot_nn(normed_ref[rows, :], up_ref[...]) + bias_ref[...])
        act = act.astype(jnp.bfloat16)
        slope = (dot_nn(cot_ref[rows, :], down_ref[...]) * slope).astype(jnp.bfloat16)
        act_ref[rows, :] = act
        slope_ref[rows, :] = slope
        grad_bias_ref[...] += jnp.sum(slope.astype(jnp.float32), axis=0, keepdims=True)
        out_ref[rows, :] += dot_nt(act, down_ref[...])
        back_ref[rows, :] += dot_nt(slope, up_ref[...])

    grad_up_ref[...] = dot_nn(normed_turned[...], slope_ref[...]).astype(grad_up_ref.dtype)
    grad_down_ref[...] = dot_nn(cot_turned[...], act_ref[...]).astype(grad_down_ref.dtype)


def mlp_pass(normed, cot, weights, bias):
    tokens, channel = normed.shape
    hidden = weights.shape[2]
    width = divisor(hidden, 128, 512)
    tile = divisor(tokens, 16, 480)
    whole = pl.BlockSpec((tokens, channel), lambda j: (0, 0))
    block = pl.BlockSpec((channel, width), lambda j: (0, j))
    line = pl.BlockSpec((1, width), lambda j: (0, j))
    part = lambda which: pl.BlockSpec((None, channel, width), lambda j: (which, 0, j))
    total = jax.ShapeDtypeStruct((tokens, channel), jnp.float32)
    grads = jax.ShapeDtypeStruct((channel, hidden), jnp.bfloat16)
    return pl.pallas_call(
        functools.partial(mlp_body, tile),
        grid=(hidden // width,),
        in_specs=[whole, whole, part(0), part(1), line],
        out_specs=[whole, whole, block, block, line],
        out_shape=[total, total, grads, grads, jax.ShapeDtypeStruct((1, hidden), jnp.float32)],
        scratch_shapes=[
            pltpu.VMEM((channel, tokens), jnp.bfloat16),
            pltpu.VMEM((channel, tokens), jnp.bfloat16),
            pltpu.VMEM((tokens, width), jnp.bfloat16),
            pltpu.VMEM((tokens, width), jnp.bfloat16),
        ],
        compiler_params=pltpu.CompilerParams(vmem_limit_bytes=56 * 1024 * 1024),
        cost_estimate=pl.CostEstimate(
            flops=12 * tokens * channel * hidden,
            bytes_accessed=8 * channel * hidden + 12 * tokens * channel,
            transcendentals=tokens * hidden,
        ),
        name="mlp_pass",
    )(normed, cot, weights, weights, bias)


def spectral_front(arrived, lat_fwd, first_pair, second_pair, bias_one, bias_two):
    spectrum = jnp.einsum(
        "pkqr,nrqmd->nkpmd", lat_fwd, arrived, preferred_element_type=jnp.float32
    ).astype(jnp.bfloat16)
    snap_local, lat_total, pair_count, mode_local, channel = spectrum.shape
    blocked = spectrum.reshape(
        snap_local, lat_total, pair_count, mode_local, BLOCKS, channel // BLOCKS
    )
    pre_one = (
        jnp.einsum("nkqmbi,pqbio->nkpmbo", blocked, first_pair, preferred_element_type=jnp.float32)
        + bias_one
    )
    act_one = jax.nn.gelu(pre_one).astype(jnp.bfloat16)
    pre_two = (
        jnp.einsum("nkqmbi,pqbio->nkpmbo", act_one, second_pair, preferred_element_type=jnp.float32)
        + bias_two
    )
    return (blocked, pre_one, act_one, pre_two)


def adamw(master, first_mom, second_mom, gradient, step_rate):
    first_next = beta_one * first_mom + (1.0 - beta_one) * gradient
    second_next = beta_two * second_mom + (1.0 - beta_two) * gradient * gradient
    fix_one = 1.0 / (1.0 - beta_one**STEP)
    fix_two = 1.0 / (1.0 - beta_two**STEP)
    direction = first_next * fix_one / (jnp.sqrt(second_next * fix_two) + adam_eps)
    master_next = master - step_rate * (direction + decay_rate * master)
    return (master_next, first_next, second_next, master_next.astype(jnp.bfloat16))


def per_device_modes(
    fields,
    cotangent,
    valid_mask,
    kept_modes,
    mlp_master,
    mlp_first,
    mlp_second,
    filter_master,
    filter_first,
    filter_second,
    small_master,
    small_first,
    small_second,
    run_stats,
):
    group_size = lax.axis_size("sp")
    snap_local, row_local, lon_total, channel = fields.shape
    lat_total = row_local * group_size
    mode_local = kept_modes.shape[1]
    mode_total = mode_local * group_size
    block_width = channel // BLOCKS
    lon_fwd, lon_inv = lon_tables(lon_total, mode_total)
    lat_fwd = lat_table(lat_total)
    mlp_w, filt_w, small_w = (
        lax.all_gather(mlp_master.astype(jnp.bfloat16), "sp", axis=1, tiled=True),
        lax.all_gather(filter_master.astype(jnp.bfloat16), "sp", axis=1, tiled=True),
        lax.all_gather(small_master.astype(jnp.bfloat16), "sp", axis=1, tiled=True),
    )
    small_f = small_w.astype(jnp.float32)
    weights = filt_w.reshape(4, BLOCKS, block_width, block_width)
    first_pair = complex_pair(weights[0], weights[1])
    second_pair = complex_pair(weights[2], weights[3])
    bias_one = small_f[4:6].reshape(2, 1, BLOCKS, block_width)
    bias_two = small_f[6:8].reshape(2, 1, BLOCKS, block_width)
    fields_float = fields.astype(jnp.float32)
    normed, norm_pull = jax.vjp(layer_norm, fields_float, small_f[0], small_f[1])
    normed_low = normed.astype(jnp.bfloat16)
    spec_lon = jnp.einsum(
        "nrld,lqm->nrqmd", normed_low, lon_fwd, preferred_element_type=jnp.float32
    ).astype(jnp.bfloat16)
    arrived = lax.all_to_all(spec_lon, "sp", split_axis=3, concat_axis=1, tiled=True)
    spectral = spectral_front(arrived, lat_fwd, first_pair, second_pair, bias_one, bias_two)
    keep_mask = kept_modes.astype(jnp.float32)[None, :, None, :, None, None]
    masked = (shrink(spectral[3]) * keep_mask).astype(jnp.bfloat16)
    masked = masked.reshape(snap_local, lat_total, 2, mode_local, channel)
    returned = jnp.einsum(
        "pkqr,nkpmd->nrqmd", lat_fwd, masked, preferred_element_type=jnp.float32
    ).astype(jnp.bfloat16)
    home_modes = lax.all_to_all(returned, "sp", split_axis=1, concat_axis=3, tiled=True)
    filtered = jnp.einsum(
        "nrqmd,qml->nrld", home_modes, lon_inv, preferred_element_type=jnp.float32
    )
    mixture = fields_float + normed + filtered
    normed_two, norm_two_pull = jax.vjp(layer_norm, mixture, small_f[2], small_f[3])
    normed_two_low = normed_two.astype(jnp.bfloat16)
    tokens = snap_local * row_local * lon_total
    passed = mlp_pass(
        normed_two_low.reshape(tokens, channel),
        cotangent.reshape(tokens, channel),
        mlp_w,
        small_f[9:].reshape(1, -1),
    )
    output = mixture + passed[0].reshape(mixture.shape) + small_f[8]
    weight_mask = valid_mask.astype(jnp.float32)[..., None]
    variables = output[..., :NVAR]
    local_sums = jnp.stack(
        [
            jnp.sum(weight_mask * variables, axis=(0, 1, 2)),
            jnp.sum(weight_mask * variables * variables, axis=(0, 1, 2)),
        ]
    )
    total_sums = lax.psum(local_sums, ("snap", "sp"))
    positions = snap_local * lax.axis_size("snap") * lat_total * lon_total
    stats_new = stat_decay * run_stats + (1.0 - stat_decay) * total_sums / positions
    cot_float = cotangent.astype(jnp.float32)
    grad_normed_two = passed[1].reshape(mixture.shape)
    grad_bias_hidden = passed[4]
    grad_mix_norm, grad_gain_two, grad_shift_two = norm_two_pull(grad_normed_two)
    grad_mixture = cot_float + grad_mix_norm
    grad_bias_out = jnp.sum(cot_float, axis=(0, 1, 2))
    grad_filtered = grad_mixture.astype(jnp.bfloat16)
    grad_home = jnp.einsum(
        "nrld,qml->nrqmd", grad_filtered, lon_inv, preferred_element_type=jnp.float32
    ).astype(jnp.bfloat16)
    grad_returned = lax.all_to_all(grad_home, "sp", split_axis=3, concat_axis=1, tiled=True)
    grad_masked = jnp.einsum(
        "pkqr,nrqmd->nkpmd", lat_fwd, grad_returned, preferred_element_type=jnp.float32
    )
    arrived_again = lax.all_to_all(spec_lon, "sp", split_axis=3, concat_axis=1, tiled=True)
    used_front = spectral_front(arrived_again, lat_fwd, first_pair, second_pair, bias_one, bias_two)
    blocked, pre_one, act_one, pre_two = used_front
    grad_two = jax.vjp(shrink, pre_two)[1](grad_masked.reshape(pre_two.shape) * keep_mask)[
        0
    ].astype(jnp.bfloat16)
    grad_bias_two = jnp.sum(grad_two.astype(jnp.float32), axis=(0, 1, 3))
    grad_second = jnp.einsum(
        "nkqmbi,nkpmbo->pqbio", act_one, grad_two, preferred_element_type=jnp.float32
    )
    grad_act = jnp.einsum(
        "nkpmbo,pqbio->nkqmbi", grad_two, second_pair, preferred_element_type=jnp.float32
    )
    grad_one = jax.vjp(jax.nn.gelu, pre_one)[1](grad_act)[0].astype(jnp.bfloat16)
    grad_bias_one = jnp.sum(grad_one.astype(jnp.float32), axis=(0, 1, 3))
    grad_first = jnp.einsum(
        "nkqmbi,nkpmbo->pqbio", blocked, grad_one, preferred_element_type=jnp.float32
    )
    grad_spectrum = jnp.einsum(
        "nkpmbo,pqbio->nkqmbi", grad_one, first_pair, preferred_element_type=jnp.float32
    ).astype(jnp.bfloat16)
    grad_spectrum = grad_spectrum.reshape(snap_local, lat_total, 2, mode_local, channel)
    grad_lon = jnp.einsum(
        "pkqr,nkpmd->nrqmd", lat_fwd, grad_spectrum, preferred_element_type=jnp.float32
    ).astype(jnp.bfloat16)
    grad_rows = lax.all_to_all(grad_lon, "sp", split_axis=1, concat_axis=3, tiled=True)
    grad_normed = grad_mixture + jnp.einsum(
        "nrqmd,lqm->nrld", grad_rows, lon_fwd, preferred_element_type=jnp.float32
    )
    grad_field_norm, grad_gain_one, grad_shift_one = norm_pull(grad_normed)
    input_grad = grad_mixture + grad_field_norm
    grad_filter = jnp.stack(
        [
            grad_first[0, 0] + grad_first[1, 1],
            grad_first[1, 0] - grad_first[0, 1],
            grad_second[0, 0] + grad_second[1, 1],
            grad_second[1, 0] - grad_second[0, 1],
        ]
    ).reshape(4, channel, block_width)
    grad_small = jnp.concatenate(
        [
            jnp.stack([grad_gain_one, grad_shift_one, grad_gain_two, grad_shift_two]),
            grad_bias_one.reshape(2, channel),
            grad_bias_two.reshape(2, channel),
            grad_bias_out[None, :],
            grad_bias_hidden.reshape(-1, channel),
        ],
        axis=0,
    )
    shares = (
        jnp.stack([
            lax.psum_scatter(part, "sp", scatter_dimension=0, tiled=True) for part in passed[2:4]
        ]),
        lax.psum_scatter(grad_filter, "sp", scatter_dimension=1, tiled=True),
        lax.psum_scatter(grad_small, "sp", scatter_dimension=1, tiled=True),
    )
    owned = (
        lax.psum(shares[0].astype(jnp.bfloat16), "snap").astype(jnp.float32),
        lax.psum(shares[1].astype(jnp.bfloat16), "snap").astype(jnp.float32),
        lax.psum(shares[2].astype(jnp.bfloat16), "snap").astype(jnp.float32),
    )
    mlp_new, mlp_first_new, mlp_second_new, mlp_copy = adamw(
        mlp_master, mlp_first, mlp_second, owned[0], rate_mlp
    )
    filter_new, filter_first_new, filter_second_new, filter_copy = adamw(
        filter_master, filter_first, filter_second, owned[1], rate_filter
    )
    small_new, small_first_new, small_second_new, small_copy = adamw(
        small_master, small_first, small_second, owned[2], rate_small
    )
    return (
        output.astype(jnp.bfloat16),
        input_grad,
        mlp_new,
        mlp_first_new,
        mlp_second_new,
        mlp_copy,
        filter_new,
        filter_first_new,
        filter_second_new,
        filter_copy,
        small_new,
        small_first_new,
        small_second_new,
        small_copy,
        stats_new,
    )


FIRST, SECOND, THIRD, FOURTH, HALF, QUARTER, LEVEL, LAST = range(8)
SCHEDULE = {
    "a": [(FIRST, 0)],
    "b": [(FIRST, 1)],
    "c0": [(SECOND, 0)],
    "d1": [(SECOND, 1), (FIRST, 2)],
    "f0": [(THIRD, 0)],
    "f1": [(SECOND, 2), (FIRST, 3)],
    "g": [(THIRD, 1)],
    "h0": [(FIRST, 4)],
    "h1": [(FOURTH, 0), (THIRD, 2)],
    ("k2", 0): [(SECOND, 3), (SECOND, 4)],
    ("m", 0): [(FOURTH, 1), (FIRST, 5)],
    ("m0", 0): [(FOURTH, 2)],
    ("m1", 0): [(HALF, 0)],
    ("k1", 1): [(THIRD, 3)],
    ("k2", 1): [(THIRD, 4)],
    ("k0", 2): [(HALF, 1)],
    ("m", 2): [(FOURTH, 3)],
    ("m1", 2): [(QUARTER, 0)],
    ("m2", 2): [(HALF, 2), (FOURTH, 4)],
    ("k0", 3): [(FOURTH, 5)],
    ("m", 3): [(LEVEL, 0), (QUARTER, 1)],
    ("k", 4): [(HALF, 3)],
    ("k2", 4): [(LEVEL, 1)],
    ("l", 4): [(QUARTER, 2)],
    ("k", 5): [(LAST, 0)],
    ("k0", 5): [(LEVEL, 2)],
    ("k1", 5): [(QUARTER, 3)],
    ("k2", 5): [(HALF, 4)],
    ("m", 5): [(LAST, 1), (LEVEL, 3)],
    "o1": [(QUARTER, 4)],
    "p1": [(HALF, 5)],
    "r": [(LAST, 2), (LEVEL, 4)],
    "t1": [(QUARTER, 5)],
    "u1": [(LAST, 3), (LAST, 4)],
    "x0": [(LEVEL, 5)],
    "z": [(LAST, 5)],
}


def lon_matrix(lon_total, mode_total, snaps, rows):
    places = np.arange(lon_total)
    orders = np.arange(mode_total)
    angles = (places[:, None] * orders[None, :] % lon_total) * (2.0 * math.pi / lon_total)
    doubling = np.where(orders == 0, 1.0, 2.0)
    scaling = 1.0 / math.sqrt(lon_total)
    forward = np.stack([np.cos(angles), -np.sin(angles)], axis=1) * scaling
    inverse = forward * doubling

    def spread(table):
        table = np.einsum(
            "ab,lx,rs->alrbsx", np.eye(snaps), table.reshape(lon_total, -1), np.eye(rows)
        )
        return table.reshape(snaps * lon_total * rows, -1).astype(ml_dtypes.bfloat16)

    return spread(forward), spread(inverse)


def lon_turn(lon_total, rows):
    turn = np.einsum("lk,rs->rlks", np.eye(lon_total), np.eye(rows))
    return turn.reshape(rows, lon_total, lon_total * rows).astype(ml_dtypes.bfloat16)


def lat_matrix(lat_total, mode_total):
    places = np.arange(lat_total)
    angles = (places[:, None] * places[None, :] % lat_total) * (2.0 * math.pi / lat_total)
    cosine, sine = np.cos(angles), np.sin(angles)
    table = np.stack([np.stack([cosine, sine], axis=1), np.stack([-sine, cosine], axis=1)])
    table = np.einsum("pkqr,ab->pakrqb", table / math.sqrt(lat_total), np.eye(mode_total))
    size = 2 * lat_total * mode_total
    return table.reshape(size, size).astype(ml_dtypes.bfloat16)


class Refs:
    pass


def block_body(names, sizes, *refs):
    g = Refs()
    for name, ref in zip(names, refs, strict=True):
        setattr(g, name, ref)
    snaps, group, parts, width = sizes
    levels = group // 2
    tokens = g.fields.shape[0] * g.fields.shape[1]
    channel = g.fields.shape[2]
    owned = channel // group
    half = width // 2
    quarter = width // snaps
    tile = tokens // 2
    short = divisor(tokens // 2, 16, 720)
    packed = g.modes.shape[2]
    strip = divisor(tokens // 2, 48, 144)
    sub = divisor(strip, 16, 48)
    low = jnp.bfloat16
    f32 = jnp.float32

    me_snap = lax.axis_index("snap")
    me_sp = lax.axis_index("sp")
    core = lax.rem(me_sp, 2)
    level = me_sp // 2

    def at(snap, sp):
        return {"snap": snap, "sp": sp}

    def sp_after(step):
        return lax.rem(me_sp + step, group)

    def sp_before(step):
        return lax.rem(me_sp + group - step, group)

    def snap_after(step):
        return lax.rem(me_snap + step, snaps)

    def snap_before(step):
        return lax.rem(me_snap + snaps - step, snaps)

    def level_after(step):
        return lax.rem(level + step, levels)

    def level_before(step):
        return lax.rem(level + levels - step, levels)

    other_core = at(me_snap, me_sp + 1 - 2 * core)

    def send(src, dst, sems, index, target):
        return pltpu.make_async_remote_copy(
            src_ref=src,
            dst_ref=dst,
            send_sem=sems[0].at[index],
            recv_sem=sems[1].at[index],
            device_id=target,
            device_id_type=pl.DeviceIdType.MESH,
        )

    half_tokens = tokens // 2

    def strips(body, first=0, count=tokens, before=None, after=None):
        @pl.loop(0, count // strip)
        def _(step):
            if before is not None:
                before(first // strip + step)
            for at_row in range(0, strip, sub):
                body(pl.ds(pl.multiple_of(first + step * strip + at_row, 16), sub))
            if after is not None:
                after(first // strip + step)

    def half_strips(body, part, **around):
        strips(body, part * half_tokens, half_tokens, **around)

    def strip_copy(near, far, sems, place, out):
        rows = pl.ds(pl.multiple_of(place * strip, strip), strip)
        ends = [near.at[rows], far.reshape(tokens, channel).at[rows]]
        if not out:
            ends.reverse()
        return pltpu.make_async_copy(*ends, sems.at[place])

    def fields_load(place):
        return strip_copy(g.fields_in, g.fields, g.fields_sem, place, False)

    def cot_load(place):
        return strip_copy(g.cot_in, g.cot, g.cot_sem, place, False)

    def out_copy(place):
        return strip_copy(g.fields_in, g.out, g.fields_sem, place, True)

    def grad_copy(place):
        return strip_copy(g.grid, g.in_grad, g.cot_sem, place, True)

    def half_rows(part):
        return slice(part * half_tokens, (part + 1) * half_tokens)

    def fold(value):
        return jnp.sum(value.reshape(-1, 8, value.shape[1]), axis=0)

    loads = {}

    def load(name, index):
        copy = pltpu.make_async_copy(getattr(g, name), getattr(g, name + "_in"), g.load_sem.at[index])
        copy.start()
        loads[name] = copy

    for index, name in enumerate(
        [name for name in names[: names.index("out")] if name not in ("mlp", "fields", "cot")]
    ):
        load(name, index)
    for copy in (fields_load, cot_load):
        for place in range(tokens // strip):
            copy(place).start()

    def master_load(part):
        return pltpu.make_async_copy(
            g.mlp.at[:, :, part * width : (part + 1) * width],
            g.mlp_part.at[part % 2],
            g.load_sem.at[len(loads) + part % 2],
        )

    master_load(0).start()
    master_load(1).start()

    barrier = pltpu.get_barrier_semaphore()
    peers = [at(me_snap, sp_after(step)) for step in range(1, group)]
    peers += [at(snap_after(step), me_sp) for step in range(1, snaps)]
    for peer in peers:
        pl.semaphore_signal(
            barrier, inc=1, device_id=peer, device_id_type=pl.DeviceIdType.MESH
        )

    loads["small"].wait()
    loads["kept"].wait()
    g.own_small[...] = jnp.zeros_like(g.own_small)
    rows_small = g.small.shape[0]
    g.own_small[0:rows_small, 0:owned] = g.small_in[...].astype(low).astype(f32)
    pairs_kept = g.kept.shape[1]
    lines = lax.broadcasted_iota(jnp.int32, (pairs_kept, pairs_kept), 0)
    places = lax.broadcasted_iota(jnp.int32, (pairs_kept, pairs_kept), 1)
    kept = jnp.where(lines == places, g.kept_in[...].astype(f32), 0.0)
    g.own_small[16:, :] = jnp.broadcast_to(
        jnp.sum(kept, axis=1, keepdims=True), (pairs_kept, g.own_small.shape[1])
    )
    pl.semaphore_wait(barrier, len(peers))

    def small_copy(step):
        return send(
            g.own_small, g.all_small.at[me_sp], (g.small_s, g.small_r), step, at(me_snap, sp_after(step))
        )

    for step in range(1, group):
        small_copy(step).start()
    g.all_small[me_sp] = g.own_small[...]

    snap_low = lax.rem(me_snap, 2)
    snap_high = me_snap // 2
    beside_low = me_snap + 1 - 2 * snap_low
    beside_high = me_snap + 2 - 4 * snap_high

    def own_quarter(part):
        odd = lax.rem(part, 2)
        return (1 - odd) * me_snap + odd * (2 * snap_low + snap_high)

    def own_place(part):
        return pl.ds(0, snaps) if part == parts - 1 else own_quarter(part)

    def half_quarters(part):
        return pl.ds(2 * (own_quarter(part) // 2), 2)

    def own_rows(sp):
        return pl.ds(pl.multiple_of(sp * owned, owned), owned)

    def spot(part):
        if isinstance(part, int):
            return part // 2 + parts // 2 * (part % 2)
        return lax.div(part, 2) + parts // 2 * lax.rem(part, 2)

    swaps = (
        (pl.ds(0, 1), own_place(0)),
        (pl.ds(3, 2), own_place(1)),
        (pl.ds(1, 2), own_place(0)),
        (pl.ds(5, 1), own_place(5)),
    )
    swapped = {0: 0, 1: 1, 2: 2, 5: 3}

    def swap_copy(batch):
        some, place = swaps[batch]
        return send(
            g.own_w.at[some, 1 - core, place],
            g.all_w.at[some, 1 - core, place, own_rows(me_sp)],
            (g.swap_s, g.swap_r),
            batch,
            other_core,
        )

    def swap_local(batch):
        some, place = swaps[batch]
        return pltpu.make_async_copy(
            g.own_w.at[some, core, place],
            g.all_w.at[some, core, place, own_rows(me_sp)],
            g.swap_l.at[batch],
        )

    def start_swap(batch):
        swap_copy(batch).start()
        swap_local(batch).start()

    def first_copy(part, step):
        rows = pl.ds(pl.multiple_of(level * 2 * owned, 2 * owned), 2 * owned)
        view = g.all_w.at[spot(part), core, own_place(part), rows]
        target = at(me_snap, 2 * level_after(step) + core)
        return send(view, view, (g.first_s, g.first_r), (part, step), target)

    def second_copy(part):
        odd = lax.rem(part, 2)
        view = g.all_w.at[spot(part), core, own_quarter(part)]
        target = at((1 - odd) * beside_low + odd * beside_high, me_sp)
        return send(view, view, (g.second_s, g.second_r), part, target)

    def third_copy(part):
        odd = lax.rem(part, 2)
        view = g.all_w.at[spot(part), core, half_quarters(part)]
        target = at((1 - odd) * beside_high + odd * beside_low, me_sp)
        return send(view, view, (g.third_s, g.third_r), part, target)

    def fourth_copy(part):
        view = g.all_w.at[spot(part), core]
        return send(view, view, (g.fourth_s, g.fourth_r), part, other_core)

    def start_first(part):
        if part in swapped:
            swap_copy(swapped[part]).wait_recv()
            swap_local(swapped[part]).wait()
        for step in range(1, levels):
            first_copy(part, step).start()

    def wait_first(part):
        for step in range(1, levels):
            first_copy(part, step).wait_recv()

    def pass_second(part):
        wait_first(part)
        second_copy(part).start()

    def pass_third(part):
        second_copy(part).wait_recv()
        third_copy(part).start()

    def pass_fourth(part):
        if part == parts - 1:
            wait_first(part)
        else:
            third_copy(part).wait_recv()
        fourth_copy(part).start()

    stages = {FIRST: start_first, SECOND: pass_second, THIRD: pass_third, FOURTH: pass_fourth}

    def reach(point):
        for stage, part in SCHEDULE.get(point, ()):
            stages[stage](part)

    for part in range(parts):
        master_load(part).wait()
        for place in range(snaps):
            cols = slice(place * quarter, (place + 1) * quarter)
            g.own_w[spot(part), :, place] = g.mlp_part[part % 2, :, :, cols].astype(low)
        if part + 2 < parts:
            master_load(part + 2).start()
        if part == 0:
            start_swap(0)
        elif part == parts - 1:
            for batch in range(1, len(swaps)):
                start_swap(batch)
    reach("a")

    def first_unit(rows):
        values = g.fields_in[rows, :].astype(f32)
        centred = values - jnp.mean(values, axis=-1, keepdims=True)
        scale = lax.rsqrt(jnp.mean(centred * centred, axis=-1, keepdims=True) + eps_norm)
        g.scale_one[rows, :] = scale
        g.grid[rows, :] = centred * scale

    strips(first_unit, before=lambda place: fields_load(place).wait())
    reach("b")
    for step in range(1, group):
        small_copy(step).wait_recv()
    for sp in range(group):
        g.gains[:, sp * owned : (sp + 1) * owned] = g.all_small[sp, 0:16, 0:owned]
        g.keep[sp * pairs_kept : (sp + 1) * pairs_kept, :] = g.all_small[sp, 16:, :]

    def first_norm(rows):
        unit = g.grid[rows, :]
        normed = unit * g.gains[0:1, :] + g.gains[1:2, :]
        g.unit_one[rows, :] = unit.astype(low)
        g.normed[rows, :] = normed.astype(low)
        g.grid[rows, :] = g.fields_in[rows, :].astype(f32) + normed

    half_snaps = g.arrived.shape[0] // 2

    third_rows = packed // 3
    spare = 128 - owned

    def pack(value):
        return jnp.concatenate(
            [
                jnp.concatenate(
                    [
                        value[at_row * third_rows : (at_row + 1) * third_rows],
                        value[packed:, at_row * spare : (at_row + 1) * spare],
                    ],
                    axis=1,
                )
                for at_row in range(3)
            ],
            axis=0,
        ).astype(low)

    def unpack(value):
        value = value.astype(f32)
        rest = [
            value[at_row * third_rows : (at_row + 1) * third_rows, owned:] for at_row in range(3)
        ]
        return jnp.concatenate([value[:, 0:owned], jnp.concatenate(rest, axis=1)], axis=0)

    def block_copy(which, part, step):
        target = sp_after(step)
        return send(
            g.modes.at[part, target],
            g.modes_got.at[part, me_sp],
            (g.block_s, g.block_r),
            (which, part, step),
            at(me_snap, target),
        )

    def row_copy(which, part, step):
        target = sp_after(step)
        return send(
            g.rows_out.at[part, target],
            g.rows_got.at[part, me_sp],
            (g.row_s, g.row_r),
            (which, part, step),
            at(me_snap, target),
        )

    def to_blocks(table, which, part):
        modes = dot_nn(table, g.normed[half_rows(part), :])
        for block in range(group):
            g.modes[part, block] = pack(modes[:, block * owned : (block + 1) * owned])
        for step in range(1, group):
            block_copy(which, part, step).start()
        g.modes_got[part, me_sp] = g.modes[part, me_sp]

    def take_blocks(which, part):
        for step in range(1, group):
            block_copy(which, part, step).wait_recv()
        each = g.arrived.shape[1] // group
        for sp in range(group):
            value = unpack(g.modes_got[part, sp])
            value = jnp.concatenate([value, jnp.zeros((value.shape[0], spare), f32)], axis=1)
            for index in range(half_snaps):
                g.arrived[part * half_snaps + index, sp * each : (sp + 1) * each, :] = value[
                    index * each : (index + 1) * each
                ].astype(low)

    def to_rows(which, part, tables):
        each = tables[0].shape[0] // group
        for sp in range(group):
            value = [table[sp * each : (sp + 1) * each, 0:owned] for table in tables]
            g.rows_out[part, sp] = pack(jnp.concatenate(value, axis=0))
        for step in range(1, group):
            row_copy(which, part, step).start()
        g.rows_got[part, me_sp] = g.rows_out[part, me_sp]

    def home_modes(which, part):
        for step in range(1, group):
            row_copy(which, part, step).wait_recv()
        for block in range(group):
            g.gathered[part, :, block * owned : (block + 1) * owned] = unpack(
                g.rows_got[part, block]
            )
        g.home_low[part] = g.gathered[part].astype(low)

    loads["lon_f"].wait()
    for part in range(2):
        half_strips(first_norm, part)
        reach("c" + str(part))
        to_blocks(g.lon_f_in[...], 0, part)
        reach("d" + str(part))

    loads["filt"].wait()
    for weight, first in ((g.weight_one, 0), (g.weight_two, 2)):
        weight[...] = jnp.zeros_like(weight)
        real = g.filt_in[first].astype(low)
        imag = g.filt_in[first + 1].astype(low)
        weight[0:owned, 0:owned] = real
        weight[128 : 128 + owned, 128 : 128 + owned] = real
        weight[0:owned, 128 : 128 + owned] = imag
        weight[128 : 128 + owned, 0:owned] = -imag

    def bias_row(first):
        return jnp.concatenate(
            [g.own_small[first : first + 1, :], g.own_small[first + 1 : first + 2, :]], axis=1
        )

    for place in range(tokens // strip):
        cot_load(place).wait()
    reach("e")
    loads["lat_f"].wait()
    loads["lat_b"].wait()
    pairs = g.arrived.shape[1] // 2
    half_modes = half_snaps * pairs

    def mode_half(part):
        return slice(part * half_modes, (part + 1) * half_modes)

    def spectra(out, kind, part):
        for snap in range(part * half_snaps, (part + 1) * half_snaps):
            spectrum = dot_nn(g.lat_f_in[...], g.arrived[snap]).astype(kind)
            rows = slice(snap * pairs, (snap + 1) * pairs)
            out[rows, 0:128] = spectrum[0:pairs]
            out[rows, 128:256] = spectrum[pairs:]

    def grids(values):
        tables = []
        for index in range(half_snaps):
            rows = values[index * pairs : (index + 1) * pairs]
            rows = jnp.concatenate([rows[:, 0:128], rows[:, 128:256]], axis=0)
            tables.append(dot_nn(g.lat_b_in[...], rows))
        return tables

    def keep_half():
        keep = jnp.concatenate([g.keep[...], g.keep[...]], axis=1)
        return jnp.concatenate([keep] * half_snaps, axis=0)

    for part in range(2):
        take_blocks(0, part)
        rows = mode_half(part)
        spectra(g.spectrum, low, part)
        g.pre_one[rows, :] = dot_nn(g.spectrum[rows, :], g.weight_one[...]) + bias_row(4)
        g.act_one[rows, :] = gelu_both(g.pre_one[rows, :])[0].astype(low)
        g.pre_two[rows, :] = dot_nn(g.act_one[rows, :], g.weight_two[...]) + bias_row(6)
        to_rows(0, part, grids((shrink(g.pre_two[rows, :]) * keep_half()).astype(low)))
        reach("f" + str(part))
    g.cot_turned[...] = g.cot_in[...].T
    reach("g")

    loads["lon_i"].wait()

    def second_norm(rows):
        values = g.grid[rows, :]
        centred = values - jnp.mean(values, axis=-1, keepdims=True)
        scale = lax.rsqrt(jnp.mean(centred * centred, axis=-1, keepdims=True) + eps_norm)
        centred = centred * scale
        g.unit_two[rows, :] = centred.astype(low)
        g.scale_two[rows, :] = scale
        g.normed[rows, :] = (centred * g.gains[2:3, :] + g.gains[3:4, :]).astype(low)
        g.grid[rows, :] = values + g.gains[8:9, :]
        g.back[rows, :] = jnp.zeros((sub, channel), f32)

    for part in range(2):
        home_modes(0, part)
        g.grid[half_rows(part), :] += dot_nn(g.lon_i_in[...], g.home_low[part])
        reach("h" + str(part))
        half_strips(second_norm, part)
        reach("i" + str(part))
    g.normed_turned[...] = g.normed[...].T
    reach("j")
    flat = jnp.concatenate([g.gains[9 + row : 10 + row, :] for row in range(rows_small - 9)], axis=1)
    for part in range(parts):
        g.bias[part] = flat[:, part * width : (part + 1) * width]

    def core_copy(part, matrix):
        slot = lax.rem(part, 2)
        return send(
            g.grads.at[matrix, :, 1 - core],
            g.core_got.at[slot, matrix],
            (g.core_s, g.core_r),
            (slot, matrix),
            other_core,
        )

    places_one = (snap_low, snap_high)
    places_two = (snap_high, snap_low)
    beside_one = (beside_low, beside_high)
    beside_two = (beside_high, beside_low)

    def half_copy(part, matrix):
        slot = lax.rem(part, 2)
        place = lax.rem(part, 4)
        return send(
            g.half_out.at[slot, matrix, 1 - places_one[matrix]],
            g.half_got.at[place, matrix],
            (g.half_s, g.half_r),
            (place, matrix),
            at(beside_one[matrix], me_sp),
        )

    def quarter_copy(part, matrix):
        slot = lax.rem(part, 2)
        return send(
            g.quarter_out.at[slot, matrix, 1 - places_two[matrix]],
            g.quarter_got.at[slot, matrix],
            (g.quarter_s, g.quarter_r),
            (slot, matrix),
            at(beside_two[matrix], me_sp),
        )

    def level_copy(part, step):
        slot = lax.rem(part, 2)
        place = lax.rem(part, 4)
        target = level_after(step)
        return send(
            g.level_out.at[slot, target],
            g.level_got.at[place, level],
            (g.level_s, g.level_r),
            (place, step),
            at(me_snap, 2 * target + core),
        )

    def last_copy(part, step):
        view = g.total.at[part, me_snap]
        return send(view, view, (g.last_s, g.last_r), (part, step), at(snap_after(step), me_sp))

    def half_stage(part):
        slot = lax.rem(part, 2)
        for matrix in range(2):

            if part >= 2:
                half_copy(part - 2, matrix).wait_send()

            core_copy(part, matrix).wait_recv()

            @pl.loop(0, levels)
            def _(row, matrix=matrix):
                both = g.grads[matrix, row, core].astype(f32) + g.core_got[
                    slot, matrix, row
                ].astype(f32)
                both = both.astype(low)
                g.half_out[slot, matrix, 0, row] = both[:, 0:half]
                g.half_out[slot, matrix, 1, row] = both[:, half:width]

            half_copy(part, matrix).start()

    def quarter_stage(part):
        slot = lax.rem(part, 2)
        for matrix in range(2):

            if part >= 2:
                quarter_copy(part - 2, matrix).wait_send()

            half_copy(part, matrix).wait_recv()
            for row in range(levels):
                both = g.half_out[slot, matrix, places_one[matrix], row].astype(f32) + g.half_got[
                    lax.rem(part, 4), matrix, row
                ].astype(f32)
                both = both.astype(low)
                g.quarter_out[slot, matrix, 0, row] = both[:, 0:quarter]
                g.quarter_out[slot, matrix, 1, row] = both[:, quarter:half]
            quarter_copy(part, matrix).start()

    def level_stage(part):
        slot = lax.rem(part, 2)

        if part >= 2:
            for step in range(1, levels):
                level_copy(part - 2, step).wait_send()

        for matrix in range(2):
            quarter_copy(part, matrix).wait_recv()
            for row in range(levels):
                both = g.quarter_out[slot, matrix, places_two[matrix], row].astype(
                    f32
                ) + g.quarter_got[slot, matrix, row].astype(f32)
                g.level_out[slot, row, matrix] = both.astype(low)
        for step in range(1, levels):
            level_copy(part, step).start()

    def last_stage(part):
        slot = lax.rem(part, 2)
        for step in range(1, levels):
            level_copy(part, step).wait_recv()
        for matrix in range(2):
            sums = g.level_out[slot, level, matrix].astype(f32)
            for step in range(1, levels):
                sums += g.level_got[lax.rem(part, 4), level_before(step), matrix].astype(f32)
            g.total[part, me_snap, matrix] = sums.astype(low)
        for step in range(1, snaps):
            last_copy(part, step).start()

    stages |= {HALF: half_stage, QUARTER: quarter_stage, LEVEL: level_stage, LAST: last_stage}

    def weight(part, matrix):
        return jnp.concatenate([g.all_w[spot(part), matrix, place] for place in range(snaps)], axis=1)

    def add_products(part, rows):
        g.grid[rows, :] += dot_nt(g.act[rows, :], weight(part, 1))
        g.back[rows, :] += dot_nt(g.slope[rows, :], weight(part, 0))

    @pl.loop(0, parts)
    def _(part):
        def reach_in(point, also=True):
            for at_part in range(parts):
                if (point, at_part) in SCHEDULE:
                    pl.when((part == at_part) & also)(functools.partial(reach, (point, at_part)))

        def tile_rows(step):
            return pl.ds(pl.multiple_of(step * tile, tile), tile)

        fourth_copy(part).wait_recv()
        reach_in("k")
        g.grad_bias[part] = jnp.zeros(g.grad_bias.shape[1:], f32)

        @pl.loop(0, tokens // tile)
        def _(step):
            rows = tile_rows(step)
            act, slope = gelu_both(dot_nn(g.normed[rows, :], weight(part, 0)) + g.bias[part])
            g.act[rows, :] = act.astype(low)
            slope = (dot_nn(g.cot_in[rows, :], weight(part, 1)) * slope).astype(low)
            g.slope[rows, :] = slope
            g.grad_bias[part] += fold(slope.astype(f32))
            for at_step in range(3):
                reach_in("k" + str(at_step), step == (at_step + 1) // 2)

        reach_in("l")

        @pl.when(part >= 1)
        def _():
            for matrix in range(2):
                core_copy(part - 1, matrix).wait_send()

        shape = g.grads.shape[1:]
        g.grads[0] = dot_nn(g.normed_turned[...], g.slope[...]).astype(low).reshape(shape)
        core_copy(part, 0).start()
        g.grads[1] = dot_nn(g.cot_turned[...], g.act[...]).astype(low).reshape(shape)
        core_copy(part, 1).start()
        reach_in("m")

        @pl.when(part < parts - 1)
        def _():
            @pl.loop(0, tokens // tile)
            def _(step):
                add_products(part, tile_rows(step))
                for at_step in range(3):
                    reach_in("m" + str(at_step), step == (at_step + 1) // 2)

    g.folds[...] = jnp.zeros_like(g.folds)

    def second_back(rows):
        grad = g.back[rows, :]
        unit = g.unit_two[rows, :].astype(f32)
        cot = g.cot_in[rows, :].astype(f32)
        pulled = grad * g.gains[2:3, :]
        middle = jnp.mean(pulled, axis=-1, keepdims=True)
        slant = jnp.mean(pulled * unit, axis=-1, keepdims=True)
        total = cot + g.scale_two[rows, :] * (pulled - middle - unit * slant)
        g.back[rows, :] = total
        g.normed[rows, :] = total.astype(low)
        g.folds[2] += fold(grad * unit)
        g.folds[3] += fold(grad)
        g.folds[4] += fold(cot)

    loads["lon_it"].wait()
    for part in range(2):

        @pl.loop(0, half_tokens // short)
        def _(step, part=part):
            first_row = part * half_tokens + step * short
            add_products(parts - 1, pl.ds(pl.multiple_of(first_row, 16), short))

        reach("o" + str(part))
        half_strips(second_back, part)
        for step in range(1, group):
            block_copy(0, part, step).wait_send()
        to_blocks(g.lon_it_in[...], 1, part)
        reach("p" + str(part))
    reach("q")

    def low_out(rows):
        g.fields_in[rows, :] = g.grid[rows, :].astype(low)

    strips(low_out, after=lambda place: out_copy(place).start())
    reach("r")
    loads["valid"].wait()
    loads["turn"].wait()
    weigh = sum(
        dot_nn(g.valid_in[:, row, :].astype(f32).astype(low), g.turn_in[row])
        for row in range(g.valid.shape[1])
    )
    places_each = weigh.shape[1]
    precise = lax.Precision.HIGHEST
    sums = [jnp.zeros((1, 128), f32), jnp.zeros((1, 128), f32)]
    for snap in range(g.valid.shape[0]):
        variables = g.grid[snap * places_each : (snap + 1) * places_each, 0:128]
        for index, value in enumerate((variables, variables * variables)):
            sums[index] += jnp.dot(
                weigh[snap : snap + 1, :], value, precision=precise, preferred_element_type=f32
            )

    reach("s")

    def dot_tn(left, right):
        return lax.dot_general(
            left, right, (((0,), (0,)), ((), ())), preferred_element_type=f32
        )

    def filter_rows(first, grad):
        g.pair_grad[...] = grad
        real = g.pair_grad[0:128, 0:128] + g.pair_grad[128:256, 128:256]
        imag = g.pair_grad[0:128, 128:256] - g.pair_grad[128:256, 0:128]
        g.filt_out[me_snap, first] = real[0:owned].astype(low)
        g.filt_out[me_snap, first + 1] = imag[0:owned].astype(low)

    for part in range(2):
        take_blocks(1, part)
        reach("t" + str(part))
        rows = mode_half(part)
        spectra(g.grad_pre, f32, part)
        bend = jnp.tanh(g.pre_two[rows, :] / shrink_level)
        grad = (g.grad_pre[rows, :] * keep_half() * (bend * bend)).astype(low)
        g.grad_two[rows, :] = grad
        grad = dot_nt(grad, g.weight_two[...]) * gelu_both(g.pre_one[rows, :])[1]
        grad = grad.astype(low)
        g.grad_one[rows, :] = grad
        for step in range(1, group):
            row_copy(0, part, step).wait_send()
        to_rows(1, part, grids(dot_nt(grad, g.weight_one[...]).astype(low)))
        reach("u" + str(part))
    reach("v")
    bias_one = jnp.sum(g.grad_one[...].astype(f32), axis=0, keepdims=True)
    bias_two = jnp.sum(g.grad_two[...].astype(f32), axis=0, keepdims=True)
    filter_rows(2, dot_tn(g.act_one[...], g.grad_two[...]))
    filter_rows(0, dot_tn(g.spectrum[...], g.grad_one[...]))

    def filter_copy(step):
        view = g.filt_out.at[me_snap]
        return send(view, view, (g.filt_s, g.filt_r), step, at(snap_after(step), me_sp))

    for step in range(1, snaps):
        filter_copy(step).start()


    reach("w")

    loads["lon_ft"].wait()

    def first_back(rows):
        grad = g.grid[rows, :]
        unit = g.unit_one[rows, :].astype(f32)
        pulled = grad * g.gains[0:1, :]
        middle = jnp.mean(pulled, axis=-1, keepdims=True)
        slant = jnp.mean(pulled * unit, axis=-1, keepdims=True)
        g.grid[rows, :] = g.back[rows, :] + g.scale_one[rows, :] * (
            pulled - middle - unit * slant
        )
        g.folds[0] += fold(grad * unit)
        g.folds[1] += fold(grad)

    for part in range(2):
        home_modes(1, part)
        reach("x" + str(part))
        g.grid[half_rows(part), :] = g.back[half_rows(part), :] + dot_nn(
            g.lon_ft_in[...], g.home_low[part]
        )
        half_strips(first_back, part, after=lambda place: grad_copy(place).start())
        reach("y" + str(part))

    g.grad_rows[...] = jnp.zeros_like(g.grad_rows)
    for index, row in enumerate((0, 1, 2, 3, 8)):
        g.grad_rows[row : row + 1, :] = jnp.sum(g.folds[index], axis=0, keepdims=True)
    flat = jnp.concatenate(
        [jnp.sum(g.grad_bias[part], axis=0, keepdims=True) for part in range(parts)], axis=1
    )
    for row in range(rows_small - 9):
        g.grad_rows[9 + row : 10 + row, :] = flat[:, row * channel : (row + 1) * channel]
    for block in range(group):
        g.tiles[block] = jnp.zeros(g.tiles.shape[1:], f32)
        g.tiles[block, :, 0:owned] = g.grad_rows[:, block * owned : (block + 1) * owned]
        g.tiles[block, 13:14, :] = sums[0]
        g.tiles[block, 14:15, :] = sums[1]

    def tile_copy(step):
        target = sp_after(step)
        return send(
            g.tiles.at[target], g.tiles_got.at[me_sp], (g.tile_s, g.tile_r), step, at(me_snap, target)
        )

    def snap_tile_copy(step):
        view = g.snap_tiles.at[me_snap]
        return send(view, view, (g.snap_tile_s, g.snap_tile_r), step, at(snap_after(step), me_sp))

    for step in range(1, group):
        tile_copy(step).start()
    reach("z")

    for batch in range(len(swaps)):
        swap_copy(batch).wait_send()
    for part in range(parts):
        if part < parts - 1:
            second_copy(part).wait_send()
            third_copy(part).wait_send()
        fourth_copy(part).wait_send()
        for step in range(1, levels):
            first_copy(part, step).wait_send()
    for step in range(1, group):
        small_copy(step).wait_send()
        for part in range(2):
            block_copy(1, part, step).wait_send()
            row_copy(1, part, step).wait_send()
    for matrix in range(2):
        core_copy(parts - 1, matrix).wait_send()
        for part in (parts - 2, parts - 1):
            half_copy(part, matrix).wait_send()
            quarter_copy(part, matrix).wait_send()
    for step in range(1, levels):
        level_copy(parts - 2, step).wait_send()
    for step in range(1, snaps):
        filter_copy(step).wait_send()

    g.tiles_got[me_sp] = g.tiles[me_sp]
    for step in range(1, group):
        tile_copy(step).wait_recv()
    tile_sum = g.tiles_got[0]
    for sp in range(1, group):
        tile_sum += g.tiles_got[sp]
    g.snap_tiles[me_snap] = tile_sum
    g.snap_tiles[me_snap, 4:5, :] = bias_one[:, 0:128]
    g.snap_tiles[me_snap, 5:6, :] = bias_one[:, 128:256]
    g.snap_tiles[me_snap, 6:7, :] = bias_two[:, 0:128]
    g.snap_tiles[me_snap, 7:8, :] = bias_two[:, 128:256]
    for step in range(1, snaps):
        snap_tile_copy(step).start()

    for step in range(1, snaps):
        filter_copy(step).wait_recv()
    filter_sum = g.filt_out[0].astype(f32)
    for snap in range(1, snaps):
        filter_sum += g.filt_out[snap].astype(f32)
    g.grad_filt[...] = filter_sum
    for part in range(parts):
        for step in range(1, snaps):
            last_copy(part, step).wait_recv()
    grads_out = pltpu.make_async_copy(g.total, g.grad_mlp, g.load_sem.at[3])
    grads_out.start()
    for step in range(1, snaps):
        snap_tile_copy(step).wait_recv()
    tile_sum = g.snap_tiles[0]
    for snap in range(1, snaps):
        tile_sum += g.snap_tiles[snap]
    g.grad_small[...] = tile_sum

    grads_out.wait()
    for place in range(tokens // strip):
        out_copy(place).wait()
        grad_copy(place).wait()
    for step in range(1, levels):
        level_copy(parts - 1, step).wait_send()
    for step in range(1, group):
        tile_copy(step).wait_send()
    for step in range(1, snaps):
        snap_tile_copy(step).wait_send()
        for part in range(parts):
            last_copy(part, step).wait_send()


def block_pass(fields, cot, valid, kept, mlp, filt, small, snaps, group):
    snap_local, row_local, lon_total, channel = fields.shape
    tokens = snap_local * row_local * lon_total
    hidden = mlp.shape[2]
    lat_total = row_local * group
    modes = kept.shape[1] * group
    owned = channel // group
    width = 512
    parts = hidden // width
    levels = group // 2
    quarter = width // snaps
    low, f32 = jnp.bfloat16, jnp.float32
    half = width // 2
    half_snaps = snap_local // 2
    lon_f, lon_i = lon_matrix(lon_total, modes, half_snaps, row_local)

    def paired(array):
        return jnp.transpose(array, (0, 2, 1, 3)).reshape(-1, row_local, channel)

    lat_f = lat_matrix(lat_total, modes)
    pair = 2 * modes * row_local
    spread = half_snaps * row_local * 2 * modes
    inputs = dict(
        small=small,
        kept=kept.T,
        fields=paired(fields),
        lon_f=jnp.asarray(np.ascontiguousarray(lon_f.T)),
        filt=filt,
        lat_f=jnp.asarray(lat_f),
        lat_b=jnp.asarray(np.ascontiguousarray(lat_f.T)),
        cot=paired(cot),
        lon_i=jnp.asarray(lon_i),
        valid=valid,
        turn=jnp.asarray(lon_turn(lon_total, row_local)),
        lon_it=jnp.asarray(np.ascontiguousarray(lon_i.T)),
        lon_ft=jnp.asarray(lon_f),
        mlp=mlp,
    )
    outputs = dict(
        out=jax.ShapeDtypeStruct((tokens // row_local, row_local, channel), low),
        in_grad=jax.ShapeDtypeStruct((tokens // row_local, row_local, channel), f32),
        grad_mlp=jax.ShapeDtypeStruct((parts, snaps, 2, owned, quarter), low),
        grad_filt=jax.ShapeDtypeStruct((4, owned, 128), f32),
        grad_small=jax.ShapeDtypeStruct((16, 128), f32),
    )
    vmem = pltpu.VMEM
    dma = pltpu.SemaphoreType.DMA
    scratch = {
        name + "_in": vmem(value.shape, value.dtype)
        for name, value in inputs.items()
        if name not in ("mlp", "fields", "cot")
    }
    strip = divisor(tokens // 2, 48, 144)
    scratch |= dict(
        mlp_part=vmem((2, 2, owned, width), f32),
        fields_in=vmem((tokens, channel), low),
        fields_sem=dma((tokens // strip,)),
        cot_sem=dma((tokens // strip,)),
        cot_in=vmem((tokens, channel), low),
        grid=vmem((tokens, channel), f32),
        back=vmem((tokens, channel), f32),
        normed=vmem((tokens, channel), low),
        normed_turned=vmem((channel, tokens), low),
        cot_turned=vmem((channel, tokens), low),
        unit_one=vmem((tokens, channel), low),
        unit_two=vmem((tokens, channel), low),
        scale_one=vmem((tokens, 1), f32),
        scale_two=vmem((tokens, 1), f32),
        own_small=vmem((16 + kept.shape[0], 128), f32),
        all_small=vmem((group, 16 + kept.shape[0], 128), f32),
        gains=vmem((16, channel), f32),
        keep=vmem((lat_total * modes, 128), f32),
        own_w=vmem((parts, 2, snaps, owned, quarter), low),
        all_w=vmem((parts, 2, snaps, channel, quarter), low),
        modes=vmem((2, group, half_snaps * pair * 3 // 4, 128), low),
        modes_got=vmem((2, group, half_snaps * pair * 3 // 4, 128), low),
        rows_out=vmem((2, group, half_snaps * pair * 3 // 4, 128), low),
        rows_got=vmem((2, group, half_snaps * pair * 3 // 4, 128), low),
        arrived=vmem((snap_local, pair * group, 128), low),
        gathered=vmem((2, spread, channel), f32),
        home_low=vmem((2, spread, channel), low),
        weight_one=vmem((256, 256), low),
        weight_two=vmem((256, 256), low),
        spectrum=vmem((snap_local * lat_total * modes, 256), low),
        pre_one=vmem((snap_local * lat_total * modes, 256), f32),
        act_one=vmem((snap_local * lat_total * modes, 256), low),
        pre_two=vmem((snap_local * lat_total * modes, 256), f32),
        grad_pre=vmem((snap_local * lat_total * modes, 256), f32),
        grad_two=vmem((snap_local * lat_total * modes, 256), low),
        grad_one=vmem((snap_local * lat_total * modes, 256), low),
        folds=vmem((5, 8, channel), f32),
        pair_grad=vmem((256, 256), f32),
        act=vmem((tokens, width), low),
        slope=vmem((tokens, width), low),
        bias=vmem((parts, 1, width), f32),
        grad_bias=vmem((parts, 8, width), f32),
        grad_rows=vmem((16, channel), f32),
        grads=vmem((2, levels, 2, owned, width), low),
        core_got=vmem((2, 2, levels, owned, width), low),
        half_out=vmem((2, 2, 2, levels, owned, half), low),
        half_got=vmem((4, 2, levels, owned, half), low),
        quarter_out=vmem((2, 2, 2, levels, owned, quarter), low),
        quarter_got=vmem((2, 2, levels, owned, quarter), low),
        level_out=vmem((2, levels, 2, owned, quarter), low),
        level_got=vmem((4, levels, 2, owned, quarter), low),
        total=vmem((parts, snaps, 2, owned, quarter), low),
        filt_out=vmem((snaps, 4, owned, 128), low),
        tiles=vmem((group, 16, 128), f32),
        tiles_got=vmem((group, 16, 128), f32),
        snap_tiles=vmem((snaps, 16, 128), f32),
        swap_l=dma((4,)),
        load_sem=dma((len(inputs) + 1,)),
    )
    for name, shape in dict(
        small=(group,),
        swap=(4,),
        first=(parts, levels),
        second=(parts,),
        third=(parts,),
        fourth=(parts,),
        block=(2, 2, group),
        row=(2, 2, group),
        core=(2, 2),
        half=(4, 2),
        quarter=(2, 2),
        level=(4, levels),
        last=(parts, snaps),
        filt=(snaps,),
        tile=(group,),
        snap_tile=(snaps,),
    ).items():
        scratch[name + "_s"] = dma(shape)
        scratch[name + "_r"] = dma(shape)
    names = [*inputs, *outputs, *scratch]
    far = pl.BlockSpec(memory_space=pl.ANY)
    near = pl.BlockSpec(memory_space=pltpu.VMEM)
    results = pl.pallas_call(
        functools.partial(block_body, names, (snaps, group, parts, width)),
        in_specs=[far] * len(inputs),
        out_specs=[far, far, far, near, near],
        out_shape=list(outputs.values()),
        scratch_shapes=list(scratch.values()),
        compiler_params=pltpu.CompilerParams(
            collective_id=0, has_side_effects=True, vmem_limit_bytes=VMEM_LIMIT
        ),
        cost_estimate=pl.CostEstimate(
            flops=12 * tokens * channel * hidden,
            bytes_accessed=4 * hidden * channel,
            transcendentals=tokens * hidden,
        ),
        name="block_pass",
    )(*inputs.values())
    return results


def adamw_near(master, first_mom, second_mom, gradient, step_rate):
    first_next = beta_one * (first_mom + gradient)
    second_next = beta_two * (second_mom + gradient * gradient)
    fix_one = 1.0 / (1.0 - beta_one**STEP)
    fix_two = 1.0 / (1.0 - beta_two**STEP)
    grown = second_next * fix_two
    bottom = grown * lax.rsqrt(grown) + adam_eps
    master_next = (1.0 - step_rate * decay_rate) * master - (
        (step_rate * fix_one) * first_next
    ) / bottom
    return (master_next, first_next, second_next, master_next.astype(jnp.bfloat16))


def step_body(names, positions, *refs):
    g = Refs()
    for name, ref in zip(names, refs, strict=True):
        setattr(g, name, ref)
    parts, snaps = g.grad_mlp.shape[:2]
    quarter = g.grad_mlp.shape[4]
    width = snaps * quarter
    chunks = g.near.shape[1]
    some = parts // chunks
    moments = ("w", "m", "v")
    results = ("new", "first", "second", "copy")

    pieces = g.far_sem.shape[2]
    ends = ((g.out, g.out_near, g.out_o), (g.in_grad, g.in_grad_near, g.in_grad_o))

    def passing(kind, piece, leg):
        size = ends[kind][0].shape[0] // pieces
        rows = pl.ds(piece * size, size)
        return pltpu.make_async_copy(
            ends[kind][leg].at[rows], ends[kind][leg + 1].at[rows], g.far_sem.at[leg, kind, piece]
        )

    through = [(kind, piece) for piece in range(pieces) for kind in range(2)]

    def chunk_cols(chunk):
        return pl.ds(chunk * some * width, some * width)

    def load(chunk):
        near = [
            pltpu.make_async_copy(
                g.grad_mlp.at[pl.ds(chunk * some, some)], g.grad_near.at[chunk], g.near_sem.at[3, chunk]
            )
        ]
        for index, kind in enumerate(moments):
            near.append(
                pltpu.make_async_copy(
                    getattr(g, "mlp_" + kind).at[:, :, chunk_cols(chunk)],
                    g.near.at[index, chunk],
                    g.near_sem.at[index, chunk],
                )
            )
        return near

    def store(chunk):
        copies = [
            pltpu.make_async_copy(
                g.near.at[index, chunk],
                getattr(g, "mlp_" + kind).at[:, :, chunk_cols(chunk)],
                g.back_sem.at[index, chunk],
            )
            for index, kind in enumerate(results[:3])
        ]
        copies.append(
            pltpu.make_async_copy(
                g.low_near.at[chunk], g.mlp_copy.at[:, :, chunk_cols(chunk)], g.back_sem.at[3, chunk]
            )
        )
        return copies

    coming = [load(chunk) for chunk in range(chunks)]
    going = [store(chunk) for chunk in range(chunks)]
    for chunk in range(chunks):
        for copy in coming[chunk]:
            copy.start()
        for each in through[chunk::chunks]:
            passing(*each, 0).start()

    def put(prefix, values):
        for kind, value in zip(results, values, strict=True):
            getattr(g, prefix + kind)[...] = value

    owned = g.filt_w.shape[2]
    put(
        "filt_",
        adamw(g.filt_w[...], g.filt_m[...], g.filt_v[...], g.grad_filt[:, :, 0:owned], rate_filter),
    )
    rows = g.small_w.shape[0]
    put(
        "small_",
        adamw(
            g.small_w[...], g.small_m[...], g.small_v[...], g.grad_small[0:rows, 0:owned], rate_small
        ),
    )
    totals = g.grad_small[rows : rows + 2, 0 : g.run.shape[1]]
    g.stats[...] = stat_decay * g.run[...] + (1.0 - stat_decay) * totals / positions

    for chunk in range(chunks):
        for copy in coming[chunk]:
            copy.wait()
        for part, matrix, snap in [
            (part, matrix, snap)
            for part in range(some)
            for matrix in range(2)
            for snap in range(snaps)
        ]:
            place = snap if matrix else 2 * (snap % 2) + snap // 2
            first_col = part * width + place * quarter
            where = (chunk, matrix, slice(None), slice(first_col, first_col + quarter))
            now = [g.near[(kind, *where)] for kind in range(3)]
            grad = g.grad_near[chunk, part, snap, matrix].astype(jnp.float32)
            values = adamw_near(*now, grad, rate_mlp)
            for kind in range(3):
                g.near[(kind, *where)] = values[kind]
            g.low_near[where] = values[3]
        for copy in going[chunk]:
            copy.start()
        for each in through[chunk::chunks]:
            passing(*each, 0).wait()
            passing(*each, 1).start()
    for each in through:
        passing(*each, 1).wait()
    for chunk in range(chunks):
        for copy in going[chunk]:
            copy.wait()


def step_pass(shown, grads, masters, run_stats, positions):
    grad_mlp, grad_filt, grad_small = grads
    mlp, filt, small = masters
    chunks = grad_mlp.shape[0]
    width = mlp[0].shape[2] // chunks
    f32, low = jnp.float32, jnp.bfloat16
    far = pl.BlockSpec(memory_space=pltpu.HBM)
    near = pl.BlockSpec(memory_space=pltpu.VMEM)
    inputs = dict(out=shown[0], in_grad=shown[1], grad_mlp=grad_mlp)
    inputs |= dict(zip(("mlp_w", "mlp_m", "mlp_v"), mlp, strict=True))
    far_in = len(inputs)
    inputs |= dict(grad_filt=grad_filt, grad_small=grad_small)
    inputs |= dict(zip(("filt_w", "filt_m", "filt_v"), filt, strict=True))
    inputs |= dict(zip(("small_w", "small_m", "small_v"), small, strict=True))
    inputs |= dict(run=run_stats)
    results = (("new", f32), ("first", f32), ("second", f32), ("copy", low))
    outputs = {
        name + "_o": jax.ShapeDtypeStruct(array.shape, array.dtype)
        for name, array in zip(("out", "in_grad"), shown, strict=True)
    }
    outputs |= {"mlp_" + kind: jax.ShapeDtypeStruct(mlp[0].shape, dt) for kind, dt in results}
    far_out = len(outputs)
    outputs |= {"filt_" + kind: jax.ShapeDtypeStruct(filt[0].shape, dt) for kind, dt in results}
    outputs |= {"small_" + kind: jax.ShapeDtypeStruct(small[0].shape, dt) for kind, dt in results}
    outputs |= dict(stats=jax.ShapeDtypeStruct(run_stats.shape, f32))
    scratch = dict(
        near=pltpu.VMEM((3, chunks, 2, mlp[0].shape[1], width), f32),
        grad_near=pltpu.VMEM((chunks, grad_mlp.shape[0] // chunks, *grad_mlp.shape[1:]), low),
        low_near=pltpu.VMEM((chunks, 2, mlp[0].shape[1], width), low),
        near_sem=pltpu.SemaphoreType.DMA((4, chunks)),
        back_sem=pltpu.SemaphoreType.DMA((4, chunks)),
        out_near=pltpu.VMEM(shown[0].shape, low),
        in_grad_near=pltpu.VMEM(shown[1].shape, f32),
        far_sem=pltpu.SemaphoreType.DMA((2, 2, divisor(shown[0].shape[0], 1, 4))),
    )
    return pl.pallas_call(
        functools.partial(step_body, [*inputs, *outputs, *scratch], positions),
        in_specs=[far] * far_in + [near] * (len(inputs) - far_in),
        out_specs=[far] * far_out + [near] * (len(outputs) - far_out),
        out_shape=list(outputs.values()),
        scratch_shapes=list(scratch.values()),
        compiler_params=pltpu.CompilerParams(vmem_limit_bytes=VMEM_LIMIT),
        name="step_pass",
    )(*inputs.values())


def per_device_blocks(
    fields,
    cotangent,
    valid_mask,
    kept_modes,
    mlp_master,
    mlp_first,
    mlp_second,
    filter_master,
    filter_first,
    filter_second,
    small_master,
    small_first,
    small_second,
    run_stats,
):
    snaps, group = lax.axis_size("snap"), lax.axis_size("sp")
    out, in_grad, *grads = block_pass(
        fields, cotangent, valid_mask, kept_modes, mlp_master, filter_master, small_master, snaps, group
    )
    snap_local, row_local, lon_total, channel = fields.shape
    positions = snap_local * snaps * row_local * group * lon_total
    out, in_grad, *stepped = step_pass(
        (out, in_grad),
        grads,
        (
            (mlp_master, mlp_first, mlp_second),
            (filter_master, filter_first, filter_second),
            (small_master, small_first, small_second),
        ),
        run_stats,
        positions,
    )
    rows_apart = (snap_local, lon_total, row_local, channel)
    out, in_grad = [
        jnp.transpose(array.reshape(rows_apart), (0, 2, 1, 3)) for array in (out, in_grad)
    ]
    return (out, in_grad, *stepped)


def per_device(*arrays):
    group, snaps = lax.axis_size("sp"), lax.axis_size("snap")
    channel, hidden = arrays[0].shape[3], arrays[4].shape[2]
    by_block = group == BLOCKS and snaps == 4 and arrays[3].shape[1] == 1
    if by_block and hidden == 6 * 512 and channel // group <= 128 and channel % (16 * group) == 0:
        return per_device_blocks(*arrays)
    return per_device_modes(*arrays)


def solution(mesh):
    return jax.shard_map(
        per_device,
        mesh=mesh,
        in_specs=(
            P("snap", "sp", None, None),
            P("snap", "sp", None, None),
            P("snap", "sp", None),
            P(None, "sp"),
            P(None, "sp", None),
            P(None, "sp", None),
            P(None, "sp", None),
            P(None, "sp", None),
            P(None, "sp", None),
            P(None, "sp", None),
            P(None, "sp"),
            P(None, "sp"),
            P(None, "sp"),
            P(),
        ),
        out_specs=(
            P("snap", "sp", None, None),
            P("snap", "sp", None, None),
            P(None, "sp", None),
            P(None, "sp", None),
            P(None, "sp", None),
            P(None, "sp", None),
            P(None, "sp", None),
            P(None, "sp", None),
            P(None, "sp", None),
            P(None, "sp", None),
            P(None, "sp"),
            P(None, "sp"),
            P(None, "sp"),
            P(None, "sp"),
            P(),
        ),
        check_vma=False,
    )
```

profile of v0, /device:TPU:0, one launch (start us, length us, event | category | flops | bytes accessed | tf_op | source)
XLA Modules:
  0.0 147.1 jit_solution(1998702649710765203)
XLA Ops:
  0.6 132.9 %block_pass.1 = (bf16[720,2,768]{2,1,0:T(2,128)(2,1)}, f32[720,2,768]{2,1,0:T(2,128)}, bf16[6,4,2,96,128]{4,3,2,1,0:T(8,128)(2,1)}, f32[4,96,128]{2,1,0:T(8,128)}, f32[16,128]{1,0:T(8,128)}) custom-call(f32[13,96]{1,0:T(8,128)} %refs_11_.2, s32[1,16]{1,0:T(1,128)} %bitcast.17, bf16[720,2,768]{2,1,0:T(2,128)(2,1)} %bitcast.14, ...), custom_call_target="tpu_custom_call" | custom-call | flops 40768634880 | bytes 9437184 | tf_op jit(solution)/shard_map/block_pass/pallas_call | solution.py:1460
  133.5 13.4 %step_pass.1 = (bf16[720,2,768]{2,1,0:T(2,128)(2,1)}, f32[720,2,768]{2,1,0:T(2,128)}, f32[2,96,3072]{2,1,0:T(8,128)}, f32[2,96,3072]{2,1,0:T(8,128)}, f32[2,96,3...) custom-call(bf16[720,2,768]{2,1,0:T(2,128)(2,1)} %get-tuple-element., ...), custom_call_target="tpu_custom_call" | custom-call | tf_op jit(solution)/shard_map/step_pass/pallas_call | solution.py:1643
where the time goes:
time: 147 us
  Pallas kernels  146 us (99%)
    pallas_call x1, Pallas kernels, block_pass(): pl.pallas_call(functools.partial(block_body, names, (snaps, group, parts,...  133 us
    pallas_call x1, Pallas kernels, step_pass(): pl.pallas_call(functools.partial(step_body, [*inputs, *outputs, *scratch]...  13.4 us

commit v1 on v0

--- a/solution.py
+++ b/solution.py
@@ -1069,16 +1069,13 @@
         reach_in("k")
         g.grad_bias[part] = jnp.zeros(g.grad_bias.shape[1:], f32)
 
-        @pl.loop(0, tokens // tile)
-        def _(step):
-            rows = tile_rows(step)
-            act, slope = gelu_both(dot_nn(g.normed[rows, :], weight(part, 0)) + g.bias[part])
-            g.act[rows, :] = act.astype(low)
-            slope = (dot_nn(g.cot_in[rows, :], weight(part, 1)) * slope).astype(low)
-            g.slope[rows, :] = slope
-            g.grad_bias[part] += fold(slope.astype(f32))
-            for at_step in range(3):
-                reach_in("k" + str(at_step), step == (at_step + 1) // 2)
+        act, slope = gelu_both(dot_nn(g.normed[...], weight(part, 0)) + g.bias[part])
+        g.act[...] = act.astype(low)
+        slope = (dot_nn(g.cot_in[...], weight(part, 1)) * slope).astype(low)
+        g.slope[...] = slope
+        g.grad_bias[part] += fold(slope.astype(f32))
+        for at_step in range(3):
+            reach_in("k" + str(at_step))
 
         reach_in("l")
 
@@ -1511,7 +1508,7 @@
             ends[kind][leg].at[rows], ends[kind][leg + 1].at[rows], g.far_sem.at[leg, kind, piece]
         )
 
-    through = [(kind, piece) for piece in range(pieces) for kind in range(2)]
+    through = [(kind, piece) for kind in range(2) for piece in range(pieces)]
 
     def chunk_cols(chunk):
         return pl.ds(chunk * some * width, some * width)
@@ -1519,17 +1516,17 @@
     def load(chunk):
         near = [
             pltpu.make_async_copy(
+                getattr(g, "mlp_" + kind).at[:, :, chunk_cols(chunk)],
+                g.near.at[index, chunk],
+                g.near_sem.at[index, chunk],
+            )
+            for index, kind in enumerate(moments)
+        ]
+        near.append(
+            pltpu.make_async_copy(
                 g.grad_mlp.at[pl.ds(chunk * some, some)], g.grad_near.at[chunk], g.near_sem.at[3, chunk]
             )
-        ]
-        for index, kind in enumerate(moments):
-            near.append(
-                pltpu.make_async_copy(
-                    getattr(g, "mlp_" + kind).at[:, :, chunk_cols(chunk)],
-                    g.near.at[index, chunk],
-                    g.near_sem.at[index, chunk],
-                )
-            )
+        )
         return near
 
     def store(chunk):

time: 147 us -> 147 us (level)
  no operation moved by 1% of the time
where the time goes in v1:
time: 147 us
  Pallas kernels  146 us (99%)
    pallas_call x1, Pallas kernels, block_pass(): pl.pallas_call(functools.partial(block_body, names, (snaps, group, parts,...  133 us
    pallas_call x1, Pallas kernels, step_pass(): pl.pallas_call(functools.partial(step_body, [*inputs, *outputs, *scratch]...  13 us

profile of v1, /device:TPU:0, one launch (start us, length us, event | category | flops | bytes accessed | tf_op | source)
XLA Modules:
  0.0 146.8 jit_solution(766382606677368573)
XLA Ops:
  0.6 133.0 %block_pass.1 = (bf16[720,2,768]{2,1,0:T(2,128)(2,1)}, f32[720,2,768]{2,1,0:T(2,128)}, bf16[6,4,2,96,128]{4,3,2,1,0:T(8,128)(2,1)}, f32[4,96,128]{2,1,0:T(8,128)}, f32[16,128]{1,0:T(8,128)}) custom-call(f32[13,96]{1,0:T(8,128)} %refs_11_.2, s32[1,16]{1,0:T(1,128)} %bitcast.17, bf16[720,2,768]{2,1,0:T(2,128)(2,1)} %bitcast.14, ...), custom_call_target="tpu_custom_call" | custom-call | flops 40768634880 | bytes 9437184 | tf_op jit(solution)/shard_map/block_pass/pallas_call | solution.py:1457
  133.7 13.0 %step_pass.1 = (bf16[720,2,768]{2,1,0:T(2,128)(2,1)}, f32[720,2,768]{2,1,0:T(2,128)}, f32[2,96,3072]{2,1,0:T(8,128)}, f32[2,96,3072]{2,1,0:T(8,128)}, f32[2,96,3...) custom-call(bf16[720,2,768]{2,1,0:T(2,128)(2,1)} %get-tuple-element., ...), custom_call_target="tpu_custom_call" | custom-call | tf_op jit(solution)/shard_map/step_pass/pallas_call | solution.py:1640
